TPU v7x, 256 devices: a whole 4x4x8 slice. The times are simulated.
256 devices in a mesh: dp: 32 (over y_hi, z, core), layer: 8 (over y_lo, x).
Axes of the slice: x: 4, y: 4 (y_hi: 2, y_lo: 2; y = y_hi * 2 + y_lo), z: 8, core: 2. Of those that a mesh axis runs over, the one named last changes fastest.
Arguments:
- activations: bfloat16 [8, 8192, 5120], P('layer', 'dp'), may hold values from -6 to 6
- backprops: bfloat16 [8, 8192, 5120], P('layer', 'dp'), may hold values from -6 to 6
- out_factors: bfloat16 [8, 32, 32, 5120], P('layer', 'dp'), may hold values from -0.078125 to 0.078125
- in_factors: bfloat16 [8, 32, 32, 5120], P('layer', 'dp'), may hold values from -0.078125 to 0.078125
- doc_lengths: int32 [32, 4], P('dp'), may hold values from 1 to 128, 256 in all within a row
Outputs:
- scores: float32 [32, 128], P('layer', 'dp')
Inputs may be any that keep to these rules, and one draw needn't show every extreme that they name: `doc_lengths`: each row holds the lengths of 4 documents that sum to 256; every row has one of length 128.
All inputs are finite; a program needn't handle non-finite values.
Results may differ from a plain program's by a relative error of at most 0.0003.
Values may be sent and summed in bfloat16 or wider, within the bound.
A program may use at most 128 MiB of HBM per device.

v0:
```python
import math

import jax
import jax.numpy as jnp
from jax import lax
from jax.sharding import PartitionSpec as P


def local(activations, backprops, out_factors, in_factors, doc_lengths):
    layers_here, tok_rows, model_width = activations.shape
    factor_rank = out_factors.shape[2]
    doc_count = doc_lengths.shape[1]
    doc_ends = jnp.cumsum(doc_lengths[0])
    doc_starts = doc_ends - doc_lengths[0]
    position = lax.iota(jnp.int32, tok_rows)
    member = (
        (position[None, :] >= doc_starts[:, None]) & (position[None, :] < doc_ends[:, None])
    ).astype(jnp.float32)
    total_queries = out_factors.shape[1] * lax.axis_size("dp")
    layers_all = layers_here * lax.axis_size("layer")
    scaling = 1.0 / math.sqrt(factor_rank * layers_all * tok_rows / doc_count)
    whole_out, whole_in = (
        lax.all_gather(out_factors, "dp", axis=1, tiled=True),
        lax.all_gather(in_factors, "dp", axis=1, tiled=True),
    )
    count_here = whole_out.shape[1]
    out_proj = lax.dot_general(
        whole_out[0].reshape(count_here * factor_rank, model_width),
        backprops[0],
        (((1,), (1,)), ((), ())),
        preferred_element_type=jnp.float32,
    )
    in_proj = lax.dot_general(
        whole_in[0].reshape(count_here * factor_rank, model_width),
        activations[0],
        (((1,), (1,)), ((), ())),
        preferred_element_type=jnp.float32,
    )
    token_terms = (out_proj * in_proj).reshape(count_here, factor_rank, tok_rows).sum(axis=1)
    summed_docs = lax.dot_general(
        token_terms, member, (((1,), (1,)), ((), ())), precision=lax.Precision.HIGHEST
    )
    score_tile = summed_docs
    score_tile = score_tile * scaling
    summed = lax.psum(score_tile, "layer")
    share_rows = total_queries // lax.axis_size("layer")
    scores = lax.dynamic_slice_in_dim(summed, lax.axis_index("layer") * share_rows, share_rows, 0)
    return scores


def solution(mesh):
    placed = (
        P("layer", "dp", None),
        P("layer", "dp", None),
        P("layer", "dp", None, None),
        P("layer", "dp", None, None),
        P("dp", None),
    )
    return jax.shard_map(
        local, mesh=mesh, in_specs=placed, out_specs=P("layer", "dp"), check_vma=False
    )
```

profile of v0, /device:TPU:8, one launch (start us, length us, event | category | flops | bytes accessed | tf_op | source)
XLA Modules:
  0.0 279.4 jit_solution(17722949150007153714)
XLA Ops:
  6.5 0.0 copy-start
  6.5 0.0 all-gather.5.cloned.1.call-start
  6.5 0.7 all-gather.5.cloned.1.call-update
  7.3 0.0 all-gather.3.cloned.1.call-start
  7.3 0.7 all-gather.3.cloned.1.call-update
  8.0 0.8 reduce-window.7
  8.8 0.7 bitcast_subtract_fusion
  9.5 111.7 %all-gather.5.cloned.1.call-done = bf16[1,32,32,5120]{3,2,0,1:T(8,128)(2,1)} async-done(((bf16[1,1,32,5120]{3,2,0,1:T(8,128)(2,1)}), bf16[1,32,32,5120]{3,2,0,1:T(8,128)(2,1)}) %all-gather.5.cloned.1.call-update) | async-done | bytes 10485776 | tf_op jit(solution)/shard_map/all_gather | solution.py:24
  121.2 0.0 copy-done
  121.2 7.9 %fusion = f32[1024,256]{1,0:T(8,128)} fusion(bf16[1024,5120]{1,0:T(8,128)(2,1)} %bitcast.26, bf16[1,256,5120]{2,1,0:T(8,128)(2,1)S(1)} %copy-done), kind=kOutput, calls=%fused_computation | convolution fusion | flops 2684354560 | bytes 14155776 | tf_op jit(solution)/shard_map/dot_general | solution.py:33
  129.1 100.7 %all-gather.3.cloned.1.call-done = bf16[1,32,32,5120]{3,2,0,1:T(8,128)(2,1)} async-done(((bf16[1,1,32,5120]{3,2,0,1:T(8,128)(2,1)}), bf16[1,32,32,5120]{3,2,0,1:T(8,128)(2,1)}) %all-gather.3.cloned.1.call-update) | async-done | bytes 10485776 | tf_op jit(solution)/shard_map/all_gather | solution.py:23
  229.8 7.9 %bitcast_reduce_fusion = f32[32,256]{1,0:T(8,128)S(1)} fusion(f32[1024,256]{1,0:T(8,128)} %fusion, bf16[1024,5120]{1,0:T(8,128)(2,1)} %bitcast.27, bf16[1,256,5120]{2,1,0:T(8,128)(2,1)} %param.6), kind=kOutput, calls=%fused_computation.6 | convolution fusion | flops 2684870656 | bytes 14188544 | tf_op jit(solution)/shard_map/dot_general | solution.py:27
  237.7 0.2 convolution_multiply_fusion
  237.9 34.1 %psum.7 = f32[32,4]{1,0:T(8,128)S(1)} all-reduce(f32[32,4]{1,0:T(8,128)S(1)} %convolution_multiply_fusion), channel_id=1, replica_groups=mesh['dp'=32,'layer'=8] {'layer'}, use_global_device_ids=true, to_apply=%region_2.3 | all-reduce | flops 128 | bytes 1024 | tf_op jit(solution)/shard_map/psum | solution.py:45
  272.0 0.6 constant_dynamic-slice_fusion
Async XLA Ops:
  6.5 114.7 %copy-start = (bf16[1,256,5120]{2,1,0:T(8,128)(2,1)S(1)}, bf16[1,256,5120]{2,1,0:T(8,128)(2,1)}, u32[]{:S(2)}) copy-start(bf16[1,256,5120]{2,1,0:T(8,128)(2,1)} %param.5) | copy-start | bytes 7864324
  6.5 114.7 %all-gather.5.cloned.1.call-start = ((), (), s32[]{:S(2)}) async-start(), calls=%async_computation.1 | async-start | bytes 10813440 | tf_op jit(solution)/shard_map/all_gather | solution.py:24
  7.3 222.5 %all-gather.3.cloned.1.call-start = ((), (), s32[]{:S(2)}) async-start(), calls=%async_computation | async-start | bytes 10813440 | tf_op jit(solution)/shard_map/all_gather | solution.py:23
Sparse Core Ops, SparseCore 0:
  10.1 111.0 all-gather.4
  124.0 105.7 all-gather.2
where the time goes:
time: 280 us; the launch traced here: 279 us
  waiting for transfers between devices  214 us (76%)
  blocking collectives  34.1 us (12%)
  matrix products  16 us (6%)
  between operations  13.4 us (5%)
    all_gather x1, waiting for transfers between devices, local(): lax.all_gather(in_factors, 'dp', axis=1, tiled=True)  112 us
    all_gather x1, waiting for transfers between devices, local(): lax.all_gather(out_factors, 'dp', axis=1, tiled=True)  101 us
    psum x1, blocking collectives, local(): summed = lax.psum(score_tile, 'layer')  34.1 us
    dot_general x1, matrix products, local(): lax.dot_general(whole_out[0].reshape(count_here * factor_rank, model_widt...  7.92 us
    dot_general x1, matrix products, local(): lax.dot_general(whole_in[0].reshape(count_here * factor_rank, model_width...  7.86 us
  transfers between devices with their start and end apart: 2, of which 2 were waited for; matrix products, arithmetic and copies ran while one was open for 3% of the time, Pallas kernels for 0%

commit v1 on v0

v1 whole, which is shorter than its diff:
```python
import functools
import math

import jax
import jax.numpy as jnp
from jax import lax
from jax.experimental import pallas as pl
from jax.experimental.pallas import tpu as pltpu
from jax.sharding import PartitionSpec as P

MESH = pl.DeviceIdType.MESH
RING = 8
LINES = 2
CORES = 2
CHUNKS = 8

SENDS = (
    ("p1", 1, 0, 0, 0, 2, 0),
    ("m1", -1, 0, 0, 0, 2, 0),
    ("y1", 0, 0, 0, 0, 2, 0),
    ("p2", 1, 0, -1, 0, 2, 1),
    ("m2", -1, 0, 1, 0, 2, 1),
    ("p5", 1, 1, 0, 0, 2, 1),
    ("m5", -1, 1, 0, 0, 2, 1),
    ("p3", 1, 0, -2, 0, 2, 2),
    ("y2", 0, 0, -2, 0, 2, 2),
    ("m3", -1, 0, 2, 0, 2, 2),
    ("y3", 0, 0, 2, 0, 2, 2),
    ("p4", 1, 0, -3, 0, 1, 3),
    ("y4", 0, 0, -3, 0, 2, 3),
    ("m4", -1, 0, 3, 1, 1, 3),
    ("y5", 0, 0, 3, 0, 2, 3),
    ("p6", 1, 1, -3, 0, 1, 4),
    ("m6", -1, 1, 3, 1, 1, 4),
)
NEEDS = {
    "p2": "p1", "m2": "m1", "p5": "y1", "p3": "p2", "m3": "m2",
    "p4": "p3", "m4": "m3", "p6": "y4", "m6": "y5",
}
LAST = ("p5", "m5", "y2", "y3", "p4", "m4", "p6", "m6")
LAST_LAG = 5
INDEX = {send[0]: i for i, send in enumerate(SENDS)}


def kernel(
    layers, lens_ref, acts_ref, grads_ref, outs_ref, ins_ref, result_ref,
    gathered, tokens, proj, member, tiles, landed,
    own_sem, tok_sem, tok_send, tok_recv, send_sem, recv_sem, mem_send, mem_recv, tile_send, tile_recv,
):
    dp, layer = lax.axis_index("dp"), lax.axis_index("layer")
    line, ring, core = dp // (RING * CORES), (dp // CORES) % RING, dp % CORES
    rank, width = outs_ref.shape[2], outs_ref.shape[3]
    count = acts_ref.shape[1]
    docs = lens_ref.shape[1]
    columns = width // CHUNKS

    def device(line_, ring_, core_):
        return (line_ * RING + ring_) * CORES + core_

    up = (device(line, (ring + 1) % RING, core), layer)
    down = (device(line, (ring + RING - 1) % RING, core), layer)
    across = (device(1 - line, ring, core), layer)
    sibling = (device(line, ring, 1 - core), layer)
    hop = {1: up, -1: down, 0: across}

    mine = pl.multiple_of((line * RING + ring) * rank, rank)
    half = pl.multiple_of(core * count, count)
    own = [
        pltpu.make_async_copy(f.at[0, 0], gathered.at[i, pl.ds(mine, rank)], own_sem.at[i])
        for i, f in enumerate((outs_ref, ins_ref))
    ]
    here = [
        pltpu.make_async_copy(t.at[0], tokens.at[i, pl.ds(half, count)], tok_sem.at[i])
        for i, t in enumerate((grads_ref, acts_ref))
    ]
    for copy in own + here:
        copy.start()

    barrier = pltpu.get_barrier_semaphore()
    for target in (up, down, across):
        pl.semaphore_signal(barrier, inc=1, device_id=target, device_id_type=MESH)
    for step in range(1, layers * CORES):
        to = (layer * CORES + core + step) % (layers * CORES)
        pl.semaphore_signal(
            barrier, inc=1, device_id=(device(line, ring, to % CORES), to // CORES), device_id_type=MESH
        )

    position = lax.broadcasted_iota(jnp.int32, (8, count), 1)
    row = lax.broadcasted_iota(jnp.int32, (8, count), 0)
    held = jnp.zeros((8, count), jnp.float32)
    first = jnp.int32(0)
    for d in range(docs):
        after = first + lens_ref[0, d]
        inside = (row == core * docs + d) & (position >= first) & (position < after)
        held = jnp.where(inside, 1.0, held)
        first = after
    member[core] = held
    proj[...] = jnp.zeros_like(proj)
    for copy in own:
        copy.wait()
    pl.semaphore_wait(barrier, 3 + layers * CORES - 1)

    def block(name, n, arriving=False):
        _, way, other, offset, part, parts, _ = SENDS[INDEX[name]]
        line_ = line if other == 0 else 1 - line
        if arriving:
            line_ = 1 - line_ if way == 0 else line_
            offset = offset - way
        slot = line_ * RING + (ring + offset + RING) % RING
        rows = pl.ds(pl.multiple_of(slot * rank, rank), rank)
        cols = pl.ds(pl.multiple_of(n * columns, columns), columns)
        return gathered.at[pl.ds(part, parts), rows, cols]

    def transfer(name, n, arriving=False):
        i = INDEX[name]
        ref = block(name, n, arriving)
        return pltpu.make_async_remote_copy(
            src_ref=ref, dst_ref=ref, send_sem=send_sem.at[i, n], recv_sem=recv_sem.at[i, n],
            device_id=hop[SENDS[i][1]], device_id_type=MESH,
        )

    def sends(lag):
        return [s[0] for s in SENDS if s[6] == lag]

    shared = [
        pltpu.make_async_remote_copy(
            src_ref=t.at[0], dst_ref=tokens.at[i, pl.ds(half, count)],
            send_sem=tok_send.at[i], recv_sem=tok_recv.at[i], device_id=sibling, device_id_type=MESH,
        )
        for i, t in enumerate((grads_ref, acts_ref))
    ]
    theirs = pltpu.make_async_remote_copy(
        src_ref=member.at[core], dst_ref=member.at[core],
        send_sem=mem_send, recv_sem=mem_recv, device_id=sibling, device_id_type=MESH,
    )

    def multiply(n):
        cols = pl.ds(pl.multiple_of(n * columns, columns), columns)

        def tile(step, carry):
            i, t = step // CORES, step % CORES
            some = pl.ds(pl.multiple_of(t * count, count), count)
            proj[i, :, some] += lax.dot_general(
                gathered[i, :, cols], tokens[i, some, cols], (((1,), (1,)), ((), ())),
                preferred_element_type=jnp.float32,
            )
            return carry

        lax.fori_loop(0, 2 * CORES, tile, 0)

    def round_of(n, carry):
        for lag in range(LAST_LAG):
            now = n - lag

            @pl.when((now >= 0) & (now < CHUNKS))
            def _():
                for name in sends(lag):
                    if name in NEEDS:
                        transfer(NEEDS[name], now, True).wait_recv()
                    transfer(name, now).start()

            if lag == 0:

                @pl.when(n == 0)
                def _():
                    for copy in shared:
                        copy.start()
                    theirs.start()

        done = n - LAST_LAG

        @pl.when(done == 0)
        def _():
            for i, copy in enumerate(here):
                copy.wait()
            other = pl.ds(pl.multiple_of((1 - core) * count, count), count)
            for i, t in enumerate((grads_ref, acts_ref)):
                pltpu.make_async_remote_copy(
                    src_ref=t.at[0], dst_ref=tokens.at[i, other],
                    send_sem=tok_send.at[i], recv_sem=tok_recv.at[i], device_id=sibling, device_id_type=MESH,
                ).wait_recv()

        @pl.when(done >= 0)
        def _():
            for name in LAST:
                transfer(name, done, True).wait_recv()
            multiply(done)

        return carry

    lax.fori_loop(0, CHUNKS + LAST_LAG, round_of, 0)

    pltpu.make_async_remote_copy(
        src_ref=member.at[1 - core], dst_ref=member.at[1 - core],
        send_sem=mem_send, recv_sem=mem_recv, device_id=sibling, device_id_type=MESH,
    ).wait_recv()
    queries = LINES * RING
    terms = (proj[0] * proj[1]).reshape(queries, rank, CORES * count).sum(axis=1)
    scores = sum(
        lax.dot_general(
            terms[:, t * count : (t + 1) * count], member[t], (((1,), (1,)), ((), ())),
            precision=lax.Precision.HIGHEST, preferred_element_type=jnp.float32,
        )
        for t in range(CORES)
    )
    each = queries // layers
    tile_row = lax.broadcasted_iota(jnp.int32, (8, scores.shape[1]), 0)
    tiles[...] = jnp.zeros_like(tiles)
    for to in range(layers):
        tile = jnp.zeros((8, scores.shape[1]), jnp.float32)
        for i in range(each):
            tile = jnp.where(tile_row == CORES * i + core, scores[to * each + i][None, :], tile)
        tiles[to, :, 0 : scores.shape[1]] = tile

    me = layer * CORES + core
    moves = []
    for step in range(1, layers * CORES):
        to = (me + step) % (layers * CORES)
        moves.append(
            pltpu.make_async_remote_copy(
                src_ref=tiles.at[to // CORES], dst_ref=landed.at[step],
                send_sem=tile_send.at[step], recv_sem=tile_recv.at[step],
                device_id=(device(line, ring, to % CORES), to // CORES), device_id_type=MESH,
            )
        )
    for move in moves:
        move.start()

    def drain(n, carry):
        for send in SENDS:
            transfer(send[0], n).wait_send()
        return carry

    lax.fori_loop(0, CHUNKS, drain, 0)
    for copy in shared:
        copy.wait_send()
    theirs.wait_send()
    total = tiles[layer]
    for step in range(1, layers * CORES):
        moves[step - 1].wait_recv()
        total = total + landed[step]
    for move in moves:
        move.wait_send()
    wide = total[0 : CORES * each]
    result_ref[...] = jnp.where(core == 0, wide[:, 0:docs], wide[:, docs : 2 * docs])


def local(activations, backprops, out_factors, in_factors, doc_lengths):
    count, width = activations.shape[1:]
    rank = out_factors.shape[2]
    docs = doc_lengths.shape[1]
    layers = lax.axis_size("layer") * activations.shape[0]
    queries = LINES * RING
    scaling = 1.0 / math.sqrt(rank * layers * count / docs)
    hbm = pl.BlockSpec(memory_space=pl.ANY)
    dma = pltpu.SemaphoreType.DMA
    flops = 2 * 2 * queries * rank * CORES * count * width
    scores = pl.pallas_call(
        functools.partial(kernel, layers),
        out_shape=jax.ShapeDtypeStruct((CORES * queries // layers, docs), jnp.float32),
        in_specs=[pl.BlockSpec(memory_space=pltpu.SMEM), hbm, hbm, hbm, hbm],
        out_specs=pl.BlockSpec(memory_space=pltpu.VMEM),
        scratch_shapes=[
            pltpu.VMEM((2, queries * rank, width), jnp.bfloat16),
            pltpu.VMEM((2, CORES * count, width), jnp.bfloat16),
            pltpu.VMEM((2, queries * rank, CORES * count), jnp.float32),
            pltpu.VMEM((CORES, 8, count), jnp.float32),
            pltpu.VMEM((layers, 8, 128), jnp.float32),
            pltpu.VMEM((layers * CORES, 8, 128), jnp.float32),
            dma((2,)),
            dma((2,)),
            dma((2,)),
            dma((2,)),
            dma((len(SENDS), CHUNKS)),
            dma((len(SENDS), CHUNKS)),
            dma,
            dma,
            dma((layers * CORES,)),
            dma((layers * CORES,)),
        ],
        compiler_params=pltpu.CompilerParams(
            collective_id=0, has_side_effects=True, vmem_limit_bytes=56 * 2**20
        ),
        cost_estimate=pl.CostEstimate(flops=flops, bytes_accessed=12 * 2**20, transcendentals=0),
        name="gather_scores",
    )(doc_lengths, activations, backprops, out_factors, in_factors)
    return scores * scaling


def solution(mesh):
    placed = (
        P("layer", "dp", None),
        P("layer", "dp", None),
        P("layer", "dp", None, None),
        P("layer", "dp", None, None),
        P("dp", None),
    )
    return jax.shard_map(
        local, mesh=mesh, in_specs=placed, out_specs=P("layer", "dp"), check_vma=False
    )
```

time: 280 us -> 99.9 us (0.36)
  waiting for transfers between devices: 214 us -> 0 us
  Pallas kernels: 0 us -> 97.3 us
  blocking collectives: 34.1 us -> 0 us
  matrix products: 16 us -> 0 us
  between operations: 13.4 us -> 0.01 us
    all_gather x2 -> x0, waiting for transfers between devices: 212 us -> none  [the longest x1 112 us: local(): lax.all_gather(in_factors, 'dp', axis=1, tiled=True)]
    pallas_call x0 -> x1, Pallas kernels: none -> 97.3 us  [local(): pl.pallas_call(functools.partial(kernel, layers), out_shape=jax.ShapeDtyp...]
    psum x1 -> x0, blocking collectives: 34.1 us -> none  [local(): summed = lax.psum(score_tile, 'layer')]
    dot_general x3 -> x0, matrix products: 16 us -> none  [the longest x1 7.92 us: local(): lax.dot_general(whole_out[0].reshape(count_here * factor_rank, model_widt...]
  transfers between devices with their start and end apart: 2 -> 0, of which waited for: 2 -> 0; matrix products, arithmetic and copies ran while one was open for 3% -> 0% of each run, Pallas kernels for 0% -> 0%
where the time goes in v1:
time: 99.9 us; the launch traced here: 98.5 us
  Pallas kernels  97.3 us (97%)
  other arithmetic  1.26 us (1%)
    pallas_call x1, Pallas kernels, local(): pl.pallas_call(functools.partial(kernel, layers), out_shape=jax.ShapeDtyp...  97.3 us

profile of v1, /device:TPU:8, one launch (start us, length us, event | category | flops | bytes accessed | tf_op | source)
XLA Modules:
  0.0 98.5 jit_solution(9147949968683116713)
XLA Ops:
  0.0 97.3 %gather_scores.1 = f32[4,4]{1,0:T(4,128)} custom-call(s32[1,4]{1,0:T(1,128)} %lens_ref.1, bf16[1,256,5120]{2,1,0:T(8,128)(2,1)} %acts_ref.1, bf16[1,256,5120]{2,1,0:T(8,128)(2,1)} %grads_ref.1, bf16[1,1,32,5120]{3,2,1,0:T(8,128)(2,1)} %outs_ref.1, bf16[1,1,32,5120]{3,2,1,0:T(8,128)(2,1)} %ins_ref.1), custom_call_target="tpu_custom_call" | custom-call | flops 5368709120 | bytes 12582912 | tf_op jit(solution)/shard_map/gather_scores/pallas_call | solution.py:258
  97.3 1.3 %broadcast_multiply_fusion = f32[4,4]{1,0:T(4,128)} fusion(f32[4,4]{1,0:T(4,128)} %gather_scores.1), kind=kLoop, calls=%fused_computation | loop fusion | flops 16 | bytes 128 | tf_op jit(solution)/shard_map/mul | solution.py:287

commit v2 on v1

--- a/solution.py
+++ b/solution.py
@@ -12,47 +12,59 @@
 RING = 8
 LINES = 2
 CORES = 2
-CHUNKS = 8
-
-SENDS = (
-    ("p1", 1, 0, 0, 0, 2, 0),
-    ("m1", -1, 0, 0, 0, 2, 0),
-    ("y1", 0, 0, 0, 0, 2, 0),
-    ("p2", 1, 0, -1, 0, 2, 1),
-    ("m2", -1, 0, 1, 0, 2, 1),
-    ("p5", 1, 1, 0, 0, 2, 1),
-    ("m5", -1, 1, 0, 0, 2, 1),
-    ("p3", 1, 0, -2, 0, 2, 2),
-    ("y2", 0, 0, -2, 0, 2, 2),
-    ("m3", -1, 0, 2, 0, 2, 2),
-    ("y3", 0, 0, 2, 0, 2, 2),
-    ("p4", 1, 0, -3, 0, 1, 3),
-    ("y4", 0, 0, -3, 0, 2, 3),
-    ("m4", -1, 0, 3, 1, 1, 3),
-    ("y5", 0, 0, 3, 0, 2, 3),
-    ("p6", 1, 1, -3, 0, 1, 4),
-    ("m6", -1, 1, 3, 1, 1, 4),
+SHARE = 6
+UNIT = 128
+SIZES = (16, 14, 10)
+
+ORDER = (
+    (0, 0, 0, 1), (-1, 0, 0, 0), (1, 0, 0, 0), (0, 0, 0, 0), (1, 0, 0, 1), (0, 0, 0, 2),
+    (-1, 0, 0, 1), (-1, 0, 1, 0), (1, 0, -1, 0), (0, 0, -1, 1), (1, 0, -1, 1), (1, 0, 0, 2),
+    (-1, 0, 1, 1), (-1, 0, 0, 2), (0, 0, -2, 0), (-1, 0, 2, 0), (1, 0, -2, 1), (0, 0, 2, 1),
+    (1, 0, -2, 0), (-1, 0, 2, 1), (1, 0, -1, 2), (-1, 0, 1, 2), (0, 0, -2, 1), (0, 0, 2, 0),
+    (1, 0, -3, 1), (-1, 1, 2, 1), (-1, 1, 0, 0), (0, 0, 3, 0), (-1, 0, 2, 2), (0, 0, -3, 0),
+    (1, 0, -2, 2), (1, 0, -3, 0), (1, 1, -2, 1), (2, 0, 0, 1), (-1, 0, 3, 0), (0, 0, 1, 1),
+    (1, 1, 0, 0), (0, 0, -3, 2), (-1, 1, 3, 1), (0, 0, 3, 2), (-1, 1, 3, 0), (1, 0, -3, 2),
+    (1, 1, -3, 1), (0, 0, -2, 2), (-1, 0, 3, 1), (2, 0, 0, 0), (1, 1, 0, 2), (0, 0, 2, 2),
+    (-1, 0, 3, 2), (2, 0, 0, 2), (1, 1, -3, 0), (1, 1, -3, 2), (-1, 1, 0, 2), (2, 1, 1, 1),
+    (2, 1, 1, 0), (-1, 1, 3, 2), (2, 0, 1, 0), (2, 1, 0, 1), (2, 0, 1, 1), (2, 0, 1, 2),
+    (2, 1, 0, 0), (2, 1, 1, 2), (2, 1, 0, 2),
 )
-NEEDS = {
-    "p2": "p1", "m2": "m1", "p5": "y1", "p3": "p2", "m3": "m2",
-    "p4": "p3", "m4": "m3", "p6": "y4", "m6": "y5",
-}
-LAST = ("p5", "m5", "y2", "y3", "p4", "m4", "p6", "m6")
-LAST_LAG = 5
-INDEX = {send[0]: i for i, send in enumerate(SENDS)}
+SENDS = tuple(item for item in ORDER if item[0] != 2)
+INDEX = {item: i for i, item in enumerate(SENDS)}
+
+
+def far(offset):
+    return RING // 2 if abs(offset) == RING // 2 else offset
+
+
+def halves(item):
+    way, _, offset, _ = item
+    if way and abs(offset - way) == RING // 2:
+        return (0,) if way == 1 else (1,)
+    return (0, 1)
+
+
+def arrival(item):
+    way, line, offset, _ = item
+    return (1 - line, far(offset)) if way == 0 else (line, far(offset - way))
+
+
+ARRIVES = {(*arrival(item), half, item[3]): item for item in SENDS for half in halves(item)}
 
 
 def kernel(
     layers, lens_ref, acts_ref, grads_ref, outs_ref, ins_ref, result_ref,
-    gathered, tokens, proj, member, tiles, landed,
+    tokens, proj, member, tiles, landed,
     own_sem, tok_sem, tok_send, tok_recv, send_sem, recv_sem, mem_send, mem_recv, tile_send, tile_recv,
+    *gathered,
 ):
     dp, layer = lax.axis_index("dp"), lax.axis_index("layer")
     line, ring, core = dp // (RING * CORES), (dp // CORES) % RING, dp % CORES
     rank, width = outs_ref.shape[2], outs_ref.shape[3]
     count = acts_ref.shape[1]
     docs = lens_ref.shape[1]
-    columns = width // CHUNKS
+    starts = [UNIT * sum(SIZES[:c]) for c in range(len(SIZES))]
+    columns = [pl.ds(start, UNIT * size) for start, size in zip(starts, SIZES)]
 
     def device(line_, ring_, core_):
         return (line_ * RING + ring_) * CORES + core_
@@ -63,10 +75,11 @@
     sibling = (device(line, ring, 1 - core), layer)
     hop = {1: up, -1: down, 0: across}
 
-    mine = pl.multiple_of((line * RING + ring) * rank, rank)
+    mine = line * RING + ring
     half = pl.multiple_of(core * count, count)
     own = [
-        pltpu.make_async_copy(f.at[0, 0], gathered.at[i, pl.ds(mine, rank)], own_sem.at[i])
+        pltpu.make_async_copy(f.at[0, 0, :, columns[c]], gathered[c].at[mine, i], own_sem.at[c, i])
+        for c in range(len(SIZES))
         for i, f in enumerate((outs_ref, ins_ref))
     ]
     here = [
@@ -95,32 +108,29 @@
         held = jnp.where(inside, 1.0, held)
         first = after
     member[core] = held
-    proj[...] = jnp.zeros_like(proj)
     for copy in own:
         copy.wait()
     pl.semaphore_wait(barrier, 3 + layers * CORES - 1)
 
-    def block(name, n, arriving=False):
-        _, way, other, offset, part, parts, _ = SENDS[INDEX[name]]
-        line_ = line if other == 0 else 1 - line
-        if arriving:
-            line_ = 1 - line_ if way == 0 else line_
-            offset = offset - way
-        slot = line_ * RING + (ring + offset + RING) % RING
-        rows = pl.ds(pl.multiple_of(slot * rank, rank), rank)
-        cols = pl.ds(pl.multiple_of(n * columns, columns), columns)
-        return gathered.at[pl.ds(part, parts), rows, cols]
-
-    def transfer(name, n, arriving=False):
-        i = INDEX[name]
-        ref = block(name, n, arriving)
+    def block(line_, offset, item):
+        part = halves(item)
+        slot = (line if line_ == 0 else 1 - line) * RING + (ring + offset + RING) % RING
+        return gathered[item[3]].at[slot, pl.ds(part[0], len(part))]
+
+    def transfer(item, ref):
+        i = INDEX[item]
         return pltpu.make_async_remote_copy(
-            src_ref=ref, dst_ref=ref, send_sem=send_sem.at[i, n], recv_sem=recv_sem.at[i, n],
-            device_id=hop[SENDS[i][1]], device_id_type=MESH,
-        )
-
-    def sends(lag):
-        return [s[0] for s in SENDS if s[6] == lag]
+            src_ref=ref, dst_ref=ref, send_sem=send_sem.at[i], recv_sem=recv_sem.at[i],
+            device_id=hop[item[0]], device_id_type=MESH,
+        )
+
+    arrived = set()
+
+    def need(line_, offset, half, c):
+        item = ARRIVES.get((line_, far(offset), half, c))
+        if item is not None and item not in arrived:
+            arrived.add(item)
+            transfer(item, block(*arrival(item), item)).wait_recv()
 
     shared = [
         pltpu.make_async_remote_copy(
@@ -134,61 +144,49 @@
         send_sem=mem_send, recv_sem=mem_recv, device_id=sibling, device_id_type=MESH,
     )
 
-    def multiply(n):
-        cols = pl.ds(pl.multiple_of(n * columns, columns), columns)
-
-        def tile(step, carry):
-            i, t = step // CORES, step % CORES
+    def multiply(line_, half, c, first):
+        rows = (line if line_ == 0 else 1 - line) * RING
+        left = gathered[c][pl.ds(rows, RING), half].reshape(RING * rank, UNIT * SIZES[c])
+        into = pl.ds(pl.multiple_of(rows * rank, RING * rank), RING * rank)
+
+        def tile(t, carry):
             some = pl.ds(pl.multiple_of(t * count, count), count)
-            proj[i, :, some] += lax.dot_general(
-                gathered[i, :, cols], tokens[i, some, cols], (((1,), (1,)), ((), ())),
+            part = lax.dot_general(
+                left, tokens[half, some, columns[c]], (((1,), (1,)), ((), ())),
                 preferred_element_type=jnp.float32,
             )
+            if first:
+                proj[half, into, some] = part
+            else:
+                proj[half, into, some] += part
             return carry
 
-        lax.fori_loop(0, 2 * CORES, tile, 0)
-
-    def round_of(n, carry):
-        for lag in range(LAST_LAG):
-            now = n - lag
-
-            @pl.when((now >= 0) & (now < CHUNKS))
-            def _():
-                for name in sends(lag):
-                    if name in NEEDS:
-                        transfer(NEEDS[name], now, True).wait_recv()
-                    transfer(name, now).start()
-
-            if lag == 0:
-
-                @pl.when(n == 0)
-                def _():
-                    for copy in shared:
-                        copy.start()
-                    theirs.start()
-
-        done = n - LAST_LAG
-
-        @pl.when(done == 0)
-        def _():
-            for i, copy in enumerate(here):
-                copy.wait()
-            other = pl.ds(pl.multiple_of((1 - core) * count, count), count)
-            for i, t in enumerate((grads_ref, acts_ref)):
-                pltpu.make_async_remote_copy(
-                    src_ref=t.at[0], dst_ref=tokens.at[i, other],
-                    send_sem=tok_send.at[i], recv_sem=tok_recv.at[i], device_id=sibling, device_id_type=MESH,
-                ).wait_recv()
-
-        @pl.when(done >= 0)
-        def _():
-            for name in LAST:
-                transfer(name, done, True).wait_recv()
-            multiply(done)
-
-        return carry
-
-    lax.fori_loop(0, CHUNKS + LAST_LAG, round_of, 0)
+        lax.fori_loop(0, CORES, tile, 0)
+
+    other = pl.ds(pl.multiple_of((1 - core) * count, count), count)
+    begun, counted = set(), set()
+    for k, item in enumerate(ORDER):
+        if k == SHARE:
+            for copy in shared:
+                copy.start()
+            theirs.start()
+        if item[0] != 2:
+            for half in halves(item):
+                need(item[1], item[2], half, item[3])
+            transfer(item, block(item[1], item[2], item)).start()
+            continue
+        _, line_, half, c = item
+        if half not in begun:
+            begun.add(half)
+            here[half].wait()
+            pltpu.make_async_remote_copy(
+                src_ref=(grads_ref, acts_ref)[half].at[0], dst_ref=tokens.at[half, other],
+                send_sem=tok_send.at[half], recv_sem=tok_recv.at[half], device_id=sibling, device_id_type=MESH,
+            ).wait_recv()
+        for offset in range(RING):
+            need(line_, offset if offset <= RING // 2 else offset - RING, half, c)
+        multiply(line_, half, c, (line_, half) not in counted)
+        counted.add((line_, half))
 
     pltpu.make_async_remote_copy(
         src_ref=member.at[1 - core], dst_ref=member.at[1 - core],
@@ -226,12 +224,8 @@
     for move in moves:
         move.start()
 
-    def drain(n, carry):
-        for send in SENDS:
-            transfer(send[0], n).wait_send()
-        return carry
-
-    lax.fori_loop(0, CHUNKS, drain, 0)
+    for item in SENDS:
+        transfer(item, block(item[1], item[2], item)).wait_send()
     for copy in shared:
         copy.wait_send()
     theirs.wait_send()
@@ -261,22 +255,22 @@
         in_specs=[pl.BlockSpec(memory_space=pltpu.SMEM), hbm, hbm, hbm, hbm],
         out_specs=pl.BlockSpec(memory_space=pltpu.VMEM),
         scratch_shapes=[
-            pltpu.VMEM((2, queries * rank, width), jnp.bfloat16),
             pltpu.VMEM((2, CORES * count, width), jnp.bfloat16),
             pltpu.VMEM((2, queries * rank, CORES * count), jnp.float32),
             pltpu.VMEM((CORES, 8, count), jnp.float32),
             pltpu.VMEM((layers, 8, 128), jnp.float32),
             pltpu.VMEM((layers * CORES, 8, 128), jnp.float32),
+            dma((len(SIZES), 2)),
             dma((2,)),
             dma((2,)),
             dma((2,)),
-            dma((2,)),
-            dma((len(SENDS), CHUNKS)),
-            dma((len(SENDS), CHUNKS)),
+            dma((len(SENDS),)),
+            dma((len(SENDS),)),
             dma,
             dma,
             dma((layers * CORES,)),
             dma((layers * CORES,)),
+            *(pltpu.VMEM((queries, 2, rank, UNIT * size), jnp.bfloat16) for size in SIZES),
         ],
         compiler_params=pltpu.CompilerParams(
             collective_id=0, has_side_effects=True, vmem_limit_bytes=56 * 2**20

time: 99.9 us -> 92.1 us (0.922)
  Pallas kernels: 97.3 us -> 89.4 us
    pallas_call x1, Pallas kernels: 97.3 us -> 89.4 us  [local(): pl.pallas_call(functools.partial(kernel, layers), out_shape=jax.ShapeDtyp...]
where the time goes in v2:
time: 92.1 us; the launch traced here: 90.7 us
  Pallas kernels  89.4 us (97%)
  other arithmetic  1.26 us (1%)
    pallas_call x1, Pallas kernels, local(): pl.pallas_call(functools.partial(kernel, layers), out_shape=jax.ShapeDtyp...  89.4 us

profile of v2, /device:TPU:8, one launch (start us, length us, event | category | flops | bytes accessed | tf_op | source)
XLA Modules:
  0.0 90.7 jit_solution(10644535407582914017)
XLA Ops:
  0.0 89.4 %gather_scores.1 = f32[4,4]{1,0:T(4,128)} custom-call(s32[1,4]{1,0:T(1,128)} %lens_ref.1, bf16[1,256,5120]{2,1,0:T(8,128)(2,1)} %acts_ref.1, bf16[1,256,5120]{2,1,0:T(8,128)(2,1)} %grads_ref.1, bf16[1,1,32,5120]{3,2,1,0:T(8,128)(2,1)} %outs_ref.1, bf16[1,1,32,5120]{3,2,1,0:T(8,128)(2,1)} %ins_ref.1), custom_call_target="tpu_custom_call" | custom-call | flops 5368709120 | bytes 12582912 | tf_op jit(solution)/shard_map/gather_scores/pallas_call | solution.py:252
  89.5 1.3 %broadcast_multiply_fusion = f32[4,4]{1,0:T(4,128)} fusion(f32[4,4]{1,0:T(4,128)} %gather_scores.1), kind=kLoop, calls=%fused_computation | loop fusion | flops 16 | bytes 128 | tf_op jit(solution)/shard_map/mul | solution.py:281

commit v3 on v2

--- a/solution.py
+++ b/solution.py
@@ -54,8 +54,8 @@
 
 def kernel(
     layers, lens_ref, acts_ref, grads_ref, outs_ref, ins_ref, result_ref,
-    tokens, proj, member, tiles, landed,
-    own_sem, tok_sem, tok_send, tok_recv, send_sem, recv_sem, mem_send, mem_recv, tile_send, tile_recv,
+    lens, tokens, proj, member, tiles, landed,
+    lens_sem, own_sem, tok_sem, tok_send, tok_recv, send_sem, recv_sem, mem_send, mem_recv, tile_send, tile_recv,
     *gathered,
 ):
     dp, layer = lax.axis_index("dp"), lax.axis_index("layer")
@@ -74,6 +74,10 @@
     across = (device(1 - line, ring, core), layer)
     sibling = (device(line, ring, 1 - core), layer)
     hop = {1: up, -1: down, 0: across}
+
+    barrier = pltpu.get_barrier_semaphore()
+    for target in (up, down, across):
+        pl.semaphore_signal(barrier, inc=1, device_id=target, device_id_type=MESH)
 
     mine = line * RING + ring
     half = pl.multiple_of(core * count, count)
@@ -86,29 +90,20 @@
         pltpu.make_async_copy(t.at[0], tokens.at[i, pl.ds(half, count)], tok_sem.at[i])
         for i, t in enumerate((grads_ref, acts_ref))
     ]
-    for copy in own + here:
+    for copy in own[:2]:
         copy.start()
-
-    barrier = pltpu.get_barrier_semaphore()
-    for target in (up, down, across):
-        pl.semaphore_signal(barrier, inc=1, device_id=target, device_id_type=MESH)
     for step in range(1, layers * CORES):
         to = (layer * CORES + core + step) % (layers * CORES)
         pl.semaphore_signal(
             barrier, inc=1, device_id=(device(line, ring, to % CORES), to // CORES), device_id_type=MESH
         )
 
-    position = lax.broadcasted_iota(jnp.int32, (8, count), 1)
-    row = lax.broadcasted_iota(jnp.int32, (8, count), 0)
-    held = jnp.zeros((8, count), jnp.float32)
-    first = jnp.int32(0)
-    for d in range(docs):
-        after = first + lens_ref[0, d]
-        inside = (row == core * docs + d) & (position >= first) & (position < after)
-        held = jnp.where(inside, 1.0, held)
-        first = after
-    member[core] = held
-    for copy in own:
+    lengths = pltpu.make_async_copy(lens_ref, lens, lens_sem)
+    lengths.start()
+    for copy in own[2:]:
+        copy.start()
+    tiles[...] = jnp.zeros_like(tiles)
+    for copy in own[:2]:
         copy.wait()
     pl.semaphore_wait(barrier, 3 + layers * CORES - 1)
 
@@ -163,14 +158,72 @@
 
         lax.fori_loop(0, CORES, tile, 0)
 
+    me, everyone = layer * CORES + core, layers * CORES
+    each = LINES * RING // layers
+    targets = RING // each
+
+    def give(to, sender):
+        return pltpu.make_async_remote_copy(
+            src_ref=tiles.at[to // CORES], dst_ref=landed.at[sender],
+            send_sem=tile_send.at[to], recv_sem=tile_recv.at[sender],
+            device_id=(device(line, ring, to % CORES), to // CORES), device_id_type=MESH,
+        )
+
+    def finish(line_, first):
+        if first:
+            pltpu.make_async_remote_copy(
+                src_ref=member.at[1 - core], dst_ref=member.at[1 - core],
+                send_sem=mem_send, recv_sem=mem_recv, device_id=sibling, device_id_type=MESH,
+            ).wait_recv()
+        which = line if line_ == 0 else 1 - line
+        rows = pl.ds(pl.multiple_of(which * RING * rank, RING * rank), RING * rank)
+        terms = (proj[0, rows] * proj[1, rows]).reshape(RING, rank, CORES * count).sum(axis=1)
+        scores = sum(
+            lax.dot_general(
+                terms[:, t * count : (t + 1) * count], member[t], (((1,), (1,)), ((), ())),
+                precision=lax.Precision.HIGHEST, preferred_element_type=jnp.float32,
+            )
+            for t in range(CORES)
+        )
+        wide = scores.shape[1]
+        by_target = scores.reshape(targets, each, wide)
+        for i in range(each):
+            for p in range(CORES):
+                tiles[pl.ds(which * targets, targets), CORES * i + p, 0:wide] = jnp.where(core == p, by_target[:, i], 0.0)
+        for k in range(targets * CORES):
+            to = which * targets * CORES + k
+
+            @pl.when(to != me)
+            def _():
+                give(to, me).start()
+
+    def members():
+        lengths.wait()
+        position = lax.broadcasted_iota(jnp.int32, (8, count), 1)
+        row = lax.broadcasted_iota(jnp.int32, (8, count), 0)
+        held = jnp.zeros((8, count), jnp.float32)
+        first = jnp.int32(0)
+        for d in range(docs):
+            after = first + lens[0, d]
+            inside = (row == core * docs + d) & (position >= first) & (position < after)
+            held = jnp.where(inside, 1.0, held)
+            first = after
+        member[core] = held
+
     other = pl.ds(pl.multiple_of((1 - core) * count, count), count)
-    begun, counted = set(), set()
+    finished = []
+    begun, counted, loaded = set(), {}, {0}
     for k, item in enumerate(ORDER):
         if k == SHARE:
-            for copy in shared:
+            for copy in here + shared:
                 copy.start()
+            members()
             theirs.start()
         if item[0] != 2:
+            if item[3] not in loaded and item[1:3] == (0, 0):
+                loaded.add(item[3])
+                for copy in own[2 * item[3] : 2 * item[3] + 2]:
+                    copy.wait()
             for half in halves(item):
                 need(item[1], item[2], half, item[3])
             transfer(item, block(item[1], item[2], item)).start()
@@ -185,44 +238,11 @@
             ).wait_recv()
         for offset in range(RING):
             need(line_, offset if offset <= RING // 2 else offset - RING, half, c)
-        multiply(line_, half, c, (line_, half) not in counted)
-        counted.add((line_, half))
-
-    pltpu.make_async_remote_copy(
-        src_ref=member.at[1 - core], dst_ref=member.at[1 - core],
-        send_sem=mem_send, recv_sem=mem_recv, device_id=sibling, device_id_type=MESH,
-    ).wait_recv()
-    queries = LINES * RING
-    terms = (proj[0] * proj[1]).reshape(queries, rank, CORES * count).sum(axis=1)
-    scores = sum(
-        lax.dot_general(
-            terms[:, t * count : (t + 1) * count], member[t], (((1,), (1,)), ((), ())),
-            precision=lax.Precision.HIGHEST, preferred_element_type=jnp.float32,
-        )
-        for t in range(CORES)
-    )
-    each = queries // layers
-    tile_row = lax.broadcasted_iota(jnp.int32, (8, scores.shape[1]), 0)
-    tiles[...] = jnp.zeros_like(tiles)
-    for to in range(layers):
-        tile = jnp.zeros((8, scores.shape[1]), jnp.float32)
-        for i in range(each):
-            tile = jnp.where(tile_row == CORES * i + core, scores[to * each + i][None, :], tile)
-        tiles[to, :, 0 : scores.shape[1]] = tile
-
-    me = layer * CORES + core
-    moves = []
-    for step in range(1, layers * CORES):
-        to = (me + step) % (layers * CORES)
-        moves.append(
-            pltpu.make_async_remote_copy(
-                src_ref=tiles.at[to // CORES], dst_ref=landed.at[step],
-                send_sem=tile_send.at[step], recv_sem=tile_recv.at[step],
-                device_id=(device(line, ring, to % CORES), to // CORES), device_id_type=MESH,
-            )
-        )
-    for move in moves:
-        move.start()
+        multiply(line_, half, c, (line_, half) not in counted.values())
+        counted[item] = (line_, half)
+        if sum(way[0] == line_ for way in counted.values()) == 2 * len(SIZES):
+            finish(line_, len(finished) == 0)
+            finished.append(line_)
 
     for item in SENDS:
         transfer(item, block(item[1], item[2], item)).wait_send()
@@ -230,13 +250,13 @@
         copy.wait_send()
     theirs.wait_send()
     total = tiles[layer]
-    for step in range(1, layers * CORES):
-        moves[step - 1].wait_recv()
-        total = total + landed[step]
-    for move in moves:
-        move.wait_send()
-    wide = total[0 : CORES * each]
-    result_ref[...] = jnp.where(core == 0, wide[:, 0:docs], wide[:, docs : 2 * docs])
+    for step in range(1, everyone):
+        give((me + step) % everyone, (me + step) % everyone).wait_recv()
+        total = total + landed[(me + step) % everyone]
+    for step in range(1, everyone):
+        give((me + step) % everyone, me).wait_send()
+    rows = total[0 : CORES * each]
+    result_ref[...] = jnp.where(core == 0, rows[:, 0:docs], rows[:, docs : 2 * docs])
 
 
 def local(activations, backprops, out_factors, in_factors, doc_lengths):
@@ -252,14 +272,16 @@
     scores = pl.pallas_call(
         functools.partial(kernel, layers),
         out_shape=jax.ShapeDtypeStruct((CORES * queries // layers, docs), jnp.float32),
-        in_specs=[pl.BlockSpec(memory_space=pltpu.SMEM), hbm, hbm, hbm, hbm],
+        in_specs=[hbm] * 5,
         out_specs=pl.BlockSpec(memory_space=pltpu.VMEM),
         scratch_shapes=[
+            pltpu.SMEM((1, docs), jnp.int32),
             pltpu.VMEM((2, CORES * count, width), jnp.bfloat16),
             pltpu.VMEM((2, queries * rank, CORES * count), jnp.float32),
             pltpu.VMEM((CORES, 8, count), jnp.float32),
             pltpu.VMEM((layers, 8, 128), jnp.float32),
             pltpu.VMEM((layers * CORES, 8, 128), jnp.float32),
+            dma,
             dma((len(SIZES), 2)),
             dma((2,)),
             dma((2,)),

time: 92.1 us -> 90.2 us (0.979); the launches traced: 90.7 us -> 89.8 us
  no operation moved by 1% of the time
where the time goes in v3:
time: 90.2 us; the launch traced here: 89.8 us
  Pallas kernels  88.6 us (98%)
  other arithmetic  1.26 us (1%)
    pallas_call x1, Pallas kernels, local(): pl.pallas_call(functools.partial(kernel, layers), out_shape=jax.ShapeDtyp...  88.6 us

profile of v3, /device:TPU:8, one launch (start us, length us, event | category | flops | bytes accessed | tf_op | source)
XLA Modules:
  0.0 89.8 jit_solution(11684522250671289181)
XLA Ops:
  0.0 88.6 %gather_scores.1 = f32[4,4]{1,0:T(4,128)} custom-call(s32[1,4]{1,0:T(1,128)} %lens_ref.1, bf16[1,256,5120]{2,1,0:T(8,128)(2,1)} %acts_ref.1, bf16[1,256,5120]{2,1,0:T(8,128)(2,1)} %grads_ref.1, bf16[1,1,32,5120]{3,2,1,0:T(8,128)(2,1)} %outs_ref.1, bf16[1,1,32,5120]{3,2,1,0:T(8,128)(2,1)} %ins_ref.1), custom_call_target="tpu_custom_call" | custom-call | flops 5368709120 | bytes 12582912 | tf_op jit(solution)/shard_map/gather_scores/pallas_call | solution.py:272
  88.6 1.3 %broadcast_multiply_fusion = f32[4,4]{1,0:T(4,128)} fusion(f32[4,4]{1,0:T(4,128)} %gather_scores.1), kind=kLoop, calls=%fused_computation | loop fusion | flops 16 | bytes 128 | tf_op jit(solution)/shard_map/mul | solution.py:303

commit v4 on v3

--- a/solution.py
+++ b/solution.py
@@ -14,20 +14,20 @@
 CORES = 2
 SHARE = 6
 UNIT = 128
-SIZES = (16, 14, 10)
+SIZES = (18, 14, 8)
 
 ORDER = (
-    (0, 0, 0, 1), (-1, 0, 0, 0), (1, 0, 0, 0), (0, 0, 0, 0), (1, 0, 0, 1), (0, 0, 0, 2),
-    (-1, 0, 0, 1), (-1, 0, 1, 0), (1, 0, -1, 0), (0, 0, -1, 1), (1, 0, -1, 1), (1, 0, 0, 2),
-    (-1, 0, 1, 1), (-1, 0, 0, 2), (0, 0, -2, 0), (-1, 0, 2, 0), (1, 0, -2, 1), (0, 0, 2, 1),
-    (1, 0, -2, 0), (-1, 0, 2, 1), (1, 0, -1, 2), (-1, 0, 1, 2), (0, 0, -2, 1), (0, 0, 2, 0),
-    (1, 0, -3, 1), (-1, 1, 2, 1), (-1, 1, 0, 0), (0, 0, 3, 0), (-1, 0, 2, 2), (0, 0, -3, 0),
-    (1, 0, -2, 2), (1, 0, -3, 0), (1, 1, -2, 1), (2, 0, 0, 1), (-1, 0, 3, 0), (0, 0, 1, 1),
-    (1, 1, 0, 0), (0, 0, -3, 2), (-1, 1, 3, 1), (0, 0, 3, 2), (-1, 1, 3, 0), (1, 0, -3, 2),
-    (1, 1, -3, 1), (0, 0, -2, 2), (-1, 0, 3, 1), (2, 0, 0, 0), (1, 1, 0, 2), (0, 0, 2, 2),
-    (-1, 0, 3, 2), (2, 0, 0, 2), (1, 1, -3, 0), (1, 1, -3, 2), (-1, 1, 0, 2), (2, 1, 1, 1),
-    (2, 1, 1, 0), (-1, 1, 3, 2), (2, 0, 1, 0), (2, 1, 0, 1), (2, 0, 1, 1), (2, 0, 1, 2),
-    (2, 1, 0, 0), (2, 1, 1, 2), (2, 1, 0, 2),
+    (0, 0, 0, 2), (0, 0, 0, 0), (1, 0, 0, 1), (-1, 0, 0, 1), (1, 0, 0, 2), (1, 0, 0, 0),
+    (-1, 0, 0, 0), (-1, 0, 1, 1), (0, 0, -1, 1), (0, 0, 1, 1), (1, 0, -1, 2), (-1, 0, 1, 0),
+    (0, 0, 0, 1), (1, 0, -1, 0), (1, 0, -1, 1), (-1, 0, 0, 2), (0, 0, 2, 1), (-1, 0, 2, 1),
+    (0, 0, 2, 0), (1, 0, -2, 0), (-1, 0, 1, 2), (1, 0, -2, 1), (-1, 1, 2, 1), (1, 0, -2, 2),
+    (0, 0, -2, 1), (0, 0, -2, 0), (0, 0, -3, 0), (-1, 0, 2, 2), (-1, 0, 2, 0), (1, 1, 0, 0),
+    (1, 0, -3, 2), (1, 0, -3, 1), (-1, 0, 3, 1), (-1, 0, 3, 2), (-1, 1, 3, 1), (-1, 0, 3, 0),
+    (0, 0, 3, 0), (1, 1, -2, 1), (2, 0, 0, 1), (1, 0, -3, 0), (0, 0, 3, 2), (1, 1, -3, 0),
+    (0, 0, -3, 2), (-1, 1, 0, 0), (2, 0, 1, 0), (0, 0, 2, 2), (1, 1, 0, 2), (2, 0, 0, 2),
+    (-1, 1, 3, 0), (2, 0, 1, 1), (0, 0, -2, 2), (2, 1, 1, 1), (2, 0, 1, 2), (-1, 1, 0, 2),
+    (-1, 1, 3, 2), (1, 1, -3, 1), (2, 1, 0, 0), (1, 1, -3, 2), (2, 0, 0, 0), (2, 1, 1, 0),
+    (2, 1, 0, 1), (2, 1, 0, 2), (2, 1, 1, 2),
 )
 SENDS = tuple(item for item in ORDER if item[0] != 2)
 INDEX = {item: i for i, item in enumerate(SENDS)}
@@ -156,7 +156,7 @@
                 proj[half, into, some] += part
             return carry
 
-        lax.fori_loop(0, CORES, tile, 0)
+        lax.fori_loop(0, CORES, tile, 0, unroll=c == len(SIZES) - 1)
 
     me, everyone = layer * CORES + core, layers * CORES
     each = LINES * RING // layers
@@ -178,18 +178,16 @@
         which = line if line_ == 0 else 1 - line
         rows = pl.ds(pl.multiple_of(which * RING * rank, RING * rank), RING * rank)
         terms = (proj[0, rows] * proj[1, rows]).reshape(RING, rank, CORES * count).sum(axis=1)
-        scores = sum(
-            lax.dot_general(
-                terms[:, t * count : (t + 1) * count], member[t], (((1,), (1,)), ((), ())),
-                precision=lax.Precision.HIGHEST, preferred_element_type=jnp.float32,
-            )
-            for t in range(CORES)
-        )
-        wide = scores.shape[1]
-        by_target = scores.reshape(targets, each, wide)
+        lane = lax.broadcasted_iota(jnp.int32, (RING, tiles.shape[2]), 1)
+        scores = jnp.zeros(lane.shape, jnp.float32)
+        for d in range(CORES * docs):
+            t = d // docs
+            mine_of = terms[:, t * count : (t + 1) * count] * member[t, d : d + 1]
+            scores = jnp.where(lane == d, mine_of.sum(axis=1, keepdims=True), scores)
+        by_target = scores.reshape(targets, each, lane.shape[1])
         for i in range(each):
             for p in range(CORES):
-                tiles[pl.ds(which * targets, targets), CORES * i + p, 0:wide] = jnp.where(core == p, by_target[:, i], 0.0)
+                tiles[pl.ds(which * targets, targets), CORES * i + p, :] = jnp.where(core == p, by_target[:, i], 0.0)
         for k in range(targets * CORES):
             to = which * targets * CORES + k
 

time: 90.2 us -> 89.2 us (0.989)
  Pallas kernels: 88.6 us -> 87.5 us
    pallas_call x1, Pallas kernels: 88.6 us -> 87.5 us  [local(): pl.pallas_call(functools.partial(kernel, layers), out_shape=jax.ShapeDtyp...]
where the time goes in v4:
time: 89.2 us; the launch traced here: 88.8 us
  Pallas kernels  87.5 us (98%)
  other arithmetic  1.26 us (1%)
    pallas_call x1, Pallas kernels, local(): pl.pallas_call(functools.partial(kernel, layers), out_shape=jax.ShapeDtyp...  87.5 us

profile of v4, /device:TPU:8, one launch (start us, length us, event | category | flops | bytes accessed | tf_op | source)
XLA Modules:
  0.0 88.8 jit_solution(5733729438123622627)
XLA Ops:
  0.0 87.5 %gather_scores.1 = f32[4,4]{1,0:T(4,128)} custom-call(s32[1,4]{1,0:T(1,128)} %lens_ref.1, bf16[1,256,5120]{2,1,0:T(8,128)(2,1)} %acts_ref.1, bf16[1,256,5120]{2,1,0:T(8,128)(2,1)} %grads_ref.1, bf16[1,1,32,5120]{3,2,1,0:T(8,128)(2,1)} %outs_ref.1, bf16[1,1,32,5120]{3,2,1,0:T(8,128)(2,1)} %ins_ref.1), custom_call_target="tpu_custom_call" | custom-call | flops 5368709120 | bytes 12582912 | tf_op jit(solution)/shard_map/gather_scores/pallas_call | solution.py:270
  87.5 1.3 %broadcast_multiply_fusion = f32[4,4]{1,0:T(4,128)} fusion(f32[4,4]{1,0:T(4,128)} %gather_scores.1), kind=kLoop, calls=%fused_computation | loop fusion | flops 16 | bytes 128 | tf_op jit(solution)/shard_map/mul | solution.py:301

commit v5 on v4

--- a/solution.py
+++ b/solution.py
@@ -54,7 +54,7 @@
 
 def kernel(
     layers, lens_ref, acts_ref, grads_ref, outs_ref, ins_ref, result_ref,
-    lens, tokens, proj, member, tiles, landed,
+    lens, shown, tokens, proj, member, tiles, landed,
     lens_sem, own_sem, tok_sem, tok_send, tok_recv, send_sem, recv_sem, mem_send, mem_recv, tile_send, tile_recv,
     *gathered,
 ):
@@ -254,7 +254,10 @@
     for step in range(1, everyone):
         give((me + step) % everyone, me).wait_send()
     rows = total[0 : CORES * each]
-    result_ref[...] = jnp.where(core == 0, rows[:, 0:docs], rows[:, docs : 2 * docs])
+    shown[...] = jnp.where(core == 0, rows[:, 0:docs], rows[:, docs : 2 * docs])
+    answer = pltpu.make_async_copy(shown, result_ref, lens_sem)
+    answer.start()
+    answer.wait()
 
 
 def local(activations, backprops, out_factors, in_factors, doc_lengths):
@@ -271,9 +274,10 @@
         functools.partial(kernel, layers),
         out_shape=jax.ShapeDtypeStruct((CORES * queries // layers, docs), jnp.float32),
         in_specs=[hbm] * 5,
-        out_specs=pl.BlockSpec(memory_space=pltpu.VMEM),
+        out_specs=hbm,
         scratch_shapes=[
             pltpu.SMEM((1, docs), jnp.int32),
+            pltpu.VMEM((CORES * queries // layers, docs), jnp.float32),
             pltpu.VMEM((2, CORES * count, width), jnp.bfloat16),
             pltpu.VMEM((2, queries * rank, CORES * count), jnp.float32),
             pltpu.VMEM((CORES, 8, count), jnp.float32),
@@ -293,7 +297,7 @@
             *(pltpu.VMEM((queries, 2, rank, UNIT * size), jnp.bfloat16) for size in SIZES),
         ],
         compiler_params=pltpu.CompilerParams(
-            collective_id=0, has_side_effects=True, vmem_limit_bytes=56 * 2**20
+            collective_id=0, has_side_effects=True, vmem_limit_bytes=55200 * 1024
         ),
         cost_estimate=pl.CostEstimate(flops=flops, bytes_accessed=12 * 2**20, transcendentals=0),
         name="gather_scores",

time: 89.2 us -> 88.6 us (level)
  no operation moved by 1% of the time
where the time goes in v5:
time: 88.6 us; the launch traced here: 88.2 us
  Pallas kernels  86.9 us (98%)
    pallas_call x1, Pallas kernels, local(): pl.pallas_call(functools.partial(kernel, layers), out_shape=jax.ShapeDtyp...  86.9 us

profile of v5, /device:TPU:8, one launch (start us, length us, event | category | flops | bytes accessed | tf_op | source)
XLA Modules:
  0.0 88.2 jit_solution(13799866224506499439)
XLA Ops:
  0.0 0.0 copy-start
  0.0 0.7 copy-done
  0.7 86.9 %gather_scores.1 = f32[4,4]{1,0:T(4,128)S(1)} custom-call(s32[1,4]{1,0:T(1,128)S(1)} %copy-done, bf16[1,256,5120]{2,1,0:T(8,128)(2,1)} %acts_ref.1, bf16[1,256,5120]{2,1,0:T(8,128)(2,1)} %grads_ref.1, bf16[1,1,32,5120]{3,2,1,0:T(8,128)(2,1)} %outs_ref.1, bf16[1,1,32,5120]{3,2,1,0:T(8,128)(2,1)} %ins_ref.1), custom_call_target="tpu_custom_call" | custom-call | flops 5368709120 | bytes 12582912 | tf_op jit(solution)/shard_map/gather_scores/pallas_call | solution.py:273
  87.6 0.6 broadcast_multiply_fusion
Async XLA Ops:
  0.0 0.7 copy-start

commit v6 on v5

--- a/solution.py
+++ b/solution.py
@@ -139,10 +139,22 @@
         send_sem=mem_send, recv_sem=mem_recv, device_id=sibling, device_id_type=MESH,
     )
 
-    def multiply(line_, half, c, first):
+    def multiply(line_, half, c, first, last):
         rows = (line if line_ == 0 else 1 - line) * RING
         left = gathered[c][pl.ds(rows, RING), half].reshape(RING * rank, UNIT * SIZES[c])
         into = pl.ds(pl.multiple_of(rows * rank, RING * rank), RING * rank)
+
+        if last:
+            terms = []
+            for t in range(CORES):
+                some = pl.ds(t * count, count)
+                part = lax.dot_general(
+                    left, tokens[half, some, columns[c]], (((1,), (1,)), ((), ())),
+                    preferred_element_type=jnp.float32,
+                )
+                both = (proj[half, into, some] + part) * proj[1 - half, into, some]
+                terms.append(both.reshape(RING, rank, count).sum(axis=1))
+            return terms
 
         def tile(t, carry):
             some = pl.ds(pl.multiple_of(t * count, count), count)
@@ -169,20 +181,18 @@
             device_id=(device(line, ring, to % CORES), to // CORES), device_id_type=MESH,
         )
 
-    def finish(line_, first):
+    def finish(line_, first, terms):
         if first:
             pltpu.make_async_remote_copy(
                 src_ref=member.at[1 - core], dst_ref=member.at[1 - core],
                 send_sem=mem_send, recv_sem=mem_recv, device_id=sibling, device_id_type=MESH,
             ).wait_recv()
         which = line if line_ == 0 else 1 - line
-        rows = pl.ds(pl.multiple_of(which * RING * rank, RING * rank), RING * rank)
-        terms = (proj[0, rows] * proj[1, rows]).reshape(RING, rank, CORES * count).sum(axis=1)
         lane = lax.broadcasted_iota(jnp.int32, (RING, tiles.shape[2]), 1)
         scores = jnp.zeros(lane.shape, jnp.float32)
         for d in range(CORES * docs):
             t = d // docs
-            mine_of = terms[:, t * count : (t + 1) * count] * member[t, d : d + 1]
+            mine_of = terms[t] * member[t, d : d + 1]
             scores = jnp.where(lane == d, mine_of.sum(axis=1, keepdims=True), scores)
         by_target = scores.reshape(targets, each, lane.shape[1])
         for i in range(each):
@@ -236,10 +246,12 @@
             ).wait_recv()
         for offset in range(RING):
             need(line_, offset if offset <= RING // 2 else offset - RING, half, c)
-        multiply(line_, half, c, (line_, half) not in counted.values())
+        first = (line_, half) not in counted.values()
         counted[item] = (line_, half)
-        if sum(way[0] == line_ for way in counted.values()) == 2 * len(SIZES):
-            finish(line_, len(finished) == 0)
+        last = sum(way[0] == line_ for way in counted.values()) == 2 * len(SIZES)
+        terms = multiply(line_, half, c, first, last)
+        if last:
+            finish(line_, len(finished) == 0, terms)
             finished.append(line_)
 
     for item in SENDS:

time: 88.6 us -> 88.6 us (level)
  no operation moved by 1% of the time
where the time goes in v6:
time: 88.6 us; the launch traced here: 88.2 us
  Pallas kernels  86.9 us (98%)
    pallas_call x1, Pallas kernels, local(): pl.pallas_call(functools.partial(kernel, layers), out_shape=jax.ShapeDtyp...  86.9 us

profile of v6, /device:TPU:8, one launch (start us, length us, event | category | flops | bytes accessed | tf_op | source)
XLA Modules:
  0.0 88.2 jit_solution(7191300497968431534)
XLA Ops:
  0.0 0.0 copy-start
  0.0 0.7 copy-done
  0.7 86.9 %gather_scores.1 = f32[4,4]{1,0:T(4,128)S(1)} custom-call(s32[1,4]{1,0:T(1,128)S(1)} %copy-done, bf16[1,256,5120]{2,1,0:T(8,128)(2,1)} %acts_ref.1, bf16[1,256,5120]{2,1,0:T(8,128)(2,1)} %grads_ref.1, bf16[1,1,32,5120]{3,2,1,0:T(8,128)(2,1)} %outs_ref.1, bf16[1,1,32,5120]{3,2,1,0:T(8,128)(2,1)} %ins_ref.1), custom_call_target="tpu_custom_call" | custom-call | flops 5368709120 | bytes 12582912 | tf_op jit(solution)/shard_map/gather_scores/pallas_call | solution.py:285
  87.6 0.6 broadcast_multiply_fusion
Async XLA Ops:
  0.0 0.7 copy-start

commit v7 on v6

--- a/solution.py
+++ b/solution.py
@@ -90,14 +90,14 @@
         pltpu.make_async_copy(t.at[0], tokens.at[i, pl.ds(half, count)], tok_sem.at[i])
         for i, t in enumerate((grads_ref, acts_ref))
     ]
-    for copy in own[:2]:
-        copy.start()
     for step in range(1, layers * CORES):
         to = (layer * CORES + core + step) % (layers * CORES)
         pl.semaphore_signal(
             barrier, inc=1, device_id=(device(line, ring, to % CORES), to // CORES), device_id_type=MESH
         )
 
+    for copy in own[:2]:
+        copy.start()
     lengths = pltpu.make_async_copy(lens_ref, lens, lens_sem)
     lengths.start()
     for copy in own[2:]:

time: 88.6 us -> 88.6 us (level)
  no operation moved by 1% of the time
where the time goes in v7:
time: 88.6 us; the launch traced here: 88.2 us
  Pallas kernels  86.9 us (98%)
    pallas_call x1, Pallas kernels, local(): pl.pallas_call(functools.partial(kernel, layers), out_shape=jax.ShapeDtyp...  86.9 us

profile of v7, /device:TPU:8, one launch (start us, length us, event | category | flops | bytes accessed | tf_op | source)
XLA Modules:
  0.0 88.2 jit_solution(12257743452488809801)
XLA Ops:
  0.0 0.0 copy-start
  0.0 0.7 copy-done
  0.7 86.9 %gather_scores.1 = f32[4,4]{1,0:T(4,128)S(1)} custom-call(s32[1,4]{1,0:T(1,128)S(1)} %copy-done, bf16[1,256,5120]{2,1,0:T(8,128)(2,1)} %acts_ref.1, bf16[1,256,5120]{2,1,0:T(8,128)(2,1)} %grads_ref.1, bf16[1,1,32,5120]{3,2,1,0:T(8,128)(2,1)} %outs_ref.1, bf16[1,1,32,5120]{3,2,1,0:T(8,128)(2,1)} %ins_ref.1), custom_call_target="tpu_custom_call" | custom-call | flops 5368709120 | bytes 12582912 | tf_op jit(solution)/shard_map/gather_scores/pallas_call | solution.py:285
  87.6 0.6 broadcast_multiply_fusion
Async XLA Ops:
  0.0 0.7 copy-start
